TPU v7x, 32 devices: a whole 2x2x4 slice. The times are simulated.
32 devices in a mesh: cases: 2 (over y), wheel: 4 (over z), inst: 4 (over x, core).
Axes of the slice: x: 2, y: 2, z: 4, core: 2. Of those that a mesh axis runs over, the one named last changes fastest.
Arguments:
- state: float32 [16, 5, 1024, 128], P('inst', None, ('cases', 'wheel')), parts along dimension 2, as said below
- slot_blade: int32 [8], P(('cases', 'wheel')), parts along dimension 0, may hold values from 0 to 3, each once
- blade_class: int32 [8], P('cases'), parts along dimension 0, may hold values from 0 to 3
- face_index: int32 [8, 2, 128], P(('cases', 'wheel')), parts along dimension 0, may hold values from 0 to 127, as said below
- class_amplitude: float32 [4], replicated, may hold values from 0.3 to 1.2
- class_phase: float32 [4], replicated, may hold values from -3.140625 to 3.140625
Outputs:
- new_state: float32 [16, 5, 1024, 128], P('inst', None, ('cases', 'wheel')), parts along dimension 2
- last_residual: float32 [16, 5, 1024, 128], P('inst', None, ('cases', 'wheel')), parts along dimension 2
There are 2 independent parts, one for each index of `cases`. A program takes and returns all parts, laid end to end along the dimension named above; an argument that names none is the same for every part. Nothing has to cross between parts.
Inputs may be any that keep to these rules, and one draw needn't show every extreme that they name: `state`: density lies in [0.8, 1.2] and pressure is positive in every cell. `slot_blade`: each blade sits in exactly one slot. face_index[s, side, k] differs from k by at most one.
All inputs are finite; a program needn't handle non-finite values.
Results may differ from a plain program's by a relative error of at most 0.0003.
Values sent between devices are 32-bit elements; how exact they have to be, the bound alone decides.
A program may use at most 64 MiB of HBM per device.

v0:
```python
import math
import jax
import jax.numpy as jnp
from jax import lax
from jax.sharding import PartitionSpec as P

INST = 16
HEAT_RATIO = 1.4
TIME_STEP = 0.05
DISSIPATION = 2.0
FREQUENCY = 0.5


def padded_2(shard, sides, width):
    for axis, dim in sides:
        size, length = (lax.axis_size(axis), shard.shape[dim])
        up = [(i, (i + 1) % size) for i in range(size)]
        down = [(j, i) for i, j in up]
        last = lax.slice_in_dim(shard, length - width, length, axis=dim)
        initial = lax.slice_in_dim(shard, 0, width, axis=dim)
        before = lax.ppermute(last, axis, up)
        after = lax.ppermute(initial, axis, down)
        shard = jnp.concatenate([before, shard, after], axis=dim)
    return shard


def fluxes(field):
    density = field[:, 0]
    axial_mom = field[:, 1]
    pitch_mom = field[:, 2]
    radial_mom = field[:, 3]
    energy = field[:, 4]
    inverse = 1.0 / density
    axial_vel = axial_mom * inverse
    pitch_vel = pitch_mom * inverse
    pressure = (HEAT_RATIO - 1.0) * (
        energy
        - 0.5 * (axial_mom * axial_mom + pitch_mom * pitch_mom + radial_mom * radial_mom) * inverse
    )
    enthalpy = energy + pressure
    axial_flux = jnp.stack(
        [
            axial_mom,
            axial_mom * axial_vel + pressure,
            pitch_mom * axial_vel,
            radial_mom * axial_vel,
            enthalpy * axial_vel,
        ],
        1,
    )
    pitch_flux = jnp.stack(
        [
            pitch_mom,
            axial_mom * pitch_vel,
            pitch_mom * pitch_vel + pressure,
            radial_mom * pitch_vel,
            enthalpy * pitch_vel,
        ],
        1,
    )
    return (axial_flux, pitch_flux)


def spectral_matrix(count):
    steps_apart = jnp.arange(count)[:, None] - jnp.arange(count)[None, :]
    apart = steps_apart != 0
    angle = jnp.where(apart, math.pi / count * steps_apart.astype(jnp.float32), 1.0)
    parity = jnp.where(steps_apart % 2 == 0, 1.0, -1.0)
    return jnp.where(apart, 0.5 * parity * jnp.cos(angle) / jnp.sin(angle), 0.0)


def face_terms(left, right, flux_left, flux_right, speed):
    return (
        0.5 * (flux_left + flux_right)
        - speed * 0.5 * (left + right)
        - 0.5 * DISSIPATION * (right - left)
    )


def local_residual(field, extended, speed, spectral):
    axial_ext, pitch_ext = fluxes(extended)
    axial_flux = axial_ext[:, :, 1:-1, :]
    axial_pad = jnp.concatenate([axial_flux[..., :1], axial_flux, axial_flux[..., -1:]], axis=3)
    field_pad = jnp.concatenate([field[..., :1], field, field[..., -1:]], axis=3)
    axial_face = face_terms(
        field_pad[..., :-1], field_pad[..., 1:], axial_pad[..., :-1], axial_pad[..., 1:], 0.0
    )
    pitch_face = face_terms(
        extended[:, :, :-1],
        extended[:, :, 1:],
        pitch_ext[:, :, :-1],
        pitch_ext[:, :, 1:],
        speed[:, None, None, None],
    )
    return (
        -(axial_face[..., 1:] - axial_face[..., :-1])
        - (pitch_face[:, :, 1:] - pitch_face[:, :, :-1])
        - FREQUENCY * spectral
    )


def body(state, slot_blade, blade_class, face_index, class_amplitude, class_phase):
    per_dev = state.shape[0]
    own_start = lax.axis_index("inst") * per_dev
    blade = slot_blade[0]
    class_id = jnp.sum(jnp.where(jnp.arange(blade_class.shape[0]) == blade, blade_class, 0))
    class_pick = jnp.arange(class_amplitude.shape[0]) == class_id
    amplitude = jnp.sum(jnp.where(class_pick, class_amplitude, 0.0))
    phase = jnp.sum(jnp.where(class_pick, class_phase, 0.0))
    matrix = spectral_matrix(INST)
    face_row = face_index[0]
    instance = (own_start + jnp.arange(per_dev)).astype(jnp.float32)
    speed = amplitude * jnp.sin(2.0 * math.pi / INST * instance + phase)
    own_rows = lax.dynamic_slice_in_dim(matrix, own_start, per_dev, 0)

    def spectral_of(field):
        return jnp.einsum(
            "nm,mvjk->nvjk",
            own_rows,
            lax.all_gather(field, "inst", axis=0, tiled=True),
            precision=lax.Precision.HIGHEST,
        )

    def residual_of(field):
        padded = padded_2(field, (("wheel", 2),), 1)
        lower = jnp.take(padded[:, :, 0, :], face_row[0], axis=2)
        upper = jnp.take(padded[:, :, -1, :], face_row[1], axis=2)
        extended = jnp.concatenate([lower[:, :, None, :], field, upper[:, :, None, :]], axis=2)
        return local_residual(field, extended, speed, spectral_of(field))

    first = state + 0.5 * TIME_STEP * residual_of(state)
    last_residual = residual_of(first)
    new_state = state + TIME_STEP * last_residual
    return (new_state, last_residual)


def solution(mesh):
    placed = (
        P("inst", None, ("cases", "wheel"), None),
        P(("cases", "wheel")),
        P("cases"),
        P(("cases", "wheel"), None, None),
        P(),
        P(),
    )
    return jax.shard_map(
        body,
        mesh=mesh,
        in_specs=placed,
        out_specs=(
            P("inst", None, ("cases", "wheel"), None),
            P("inst", None, ("cases", "wheel"), None),
        ),
        check_vma=False,
    )
```

profile of v0, /device:TPU:0, one launch (start us, length us, event | category | flops | bytes accessed | tf_op | source)
XLA Modules:
  0.0 127.6 jit_solution(13102067222919137972)
XLA Ops:
  7.2 0.7 all-gather.3.cloned.1.call-update
  8.0 0.9 fusion.54
  8.9 3.1 %collective-permute-start = (f32[4,5,1,128]{3,2,1,0:T(1,128)S(1)}, f32[4,5,1,128]{3,2,1,0:T(1,128)S(1)}, u32[]{:S(2)}, u32[]{:S(2)}) collective-permute-start(f32[4,5,1,128]{3,2,1,0:T(1,128)S(1)} %get-tuple-element.43), channel_id=1, source_target_pairs={{0,4},{4,8},{8,12},{12,0},{1,5},{5,9},{9,13},{13,1},{2,6},{6,10},{... | collective-permute-start | bytes 30728 | tf_op jit(solution)/shard_map/ppermute | solution.py:21
  12.0 2.1 %collective-permute-start.1 = (f32[4,5,1,128]{3,2,1,0:T(1,128)S(1)}, f32[4,5,1,128]{3,2,1,0:T(1,128)S(1)}, u32[]{:S(2)}, u32[]{:S(2)}) collective-permute-start(f32[4,5,1,128]{3,2,1,0:T(1,128)S(1)} %get-tuple-element.44), channel_id=1, source_target_pairs={{4,0},{8,4},{12,8},{0,12},{5,1},{9,5},{13,9},{1,13},{6,2},{10,6},{... | collective-permute-start | bytes 30728 | tf_op jit(solution)/shard_map/ppermute | solution.py:22
  14.1 0.8 copy.63
  15.7 0.6 fusion.46
  16.3 1.3 %fusion.44 = f32[]{:T(128)} fusion(f32[4]{0:T(128)S(1)} %copy-done.7, s32[]{:T(128)} %fusion.46), kind=kLoop, calls=%fused_computation.106 | loop fusion | flops 11 | bytes 24 | tf_op jit(solution)/shard_map/reduce_sum | solution.py:108
  17.6 1.3 fusion.45
  18.9 2.2 %fusion.53 = (f32[4,5,128,1]{3,0,2,1:T(4,128)}, f32[4,5,128,1]{3,0,2,1:T(4,128)}) fusion(f32[4,5,128,128]{3,0,2,1:T(4,128)S(1)} %copy.63), kind=kLoop, calls=%fused_computation.114 | loop fusion | bytes 40960 | tf_op jit(solution)/shard_map/slice | solution.py:84
  21.2 1.3 %multiply_multiply_fusion = f32[4]{0:T(128)S(1)} fusion(f32[]{:T(128)} %fusion.45, s32[]{:T(128)S(6)} %mul.290, f32[]{:T(128)} %fusion.44), kind=kLoop, calls=%fused_computation.109 | loop fusion | flops 24 | bytes 28 | tf_op jit(solution)/shard_map/mul | solution.py:75
  22.7 0.8 gather_fusion
  23.8 0.8 gather_fusion.1
  24.7 0.3 pad_maximum_fusion.4
  26.2 0.7 fusion.50
  27.0 1.9 %fusion.30 = f32[4,5,129,128]{3,0,2,1:T(4,128)} fusion(f32[4,5,130,128]{3,0,2,1:T(4,128)S(1)} %multiply_dynamic-update-slice_fusion.6, f32[4,5,1,128]{3,0,2,1:T(4,128)S(1)} %select_bitcast_fusion.2, f32[4,5,128,128]{3,0,2,1:T(4,128)S(1)} %copy.63, f32[4,5,1,128]{3,0,2,1:T(4,128)S(1)} %select_bitcast_fusion.3, f32[4]{0:T(128)S(1)} %multiply_multiply_fusion), kind=kLoop, calls=%fused_computation.34 | loop fusion | flops 2972160 | bytes 5294096 | tf_op jit(solution)/shard_map/sub | solution.py:74
  28.9 4.3 %fusion.6 = f32[4,5,128,129]{3,0,2,1:T(4,128)} fusion(f32[4,5,128,128]{3,0,2,1:T(4,128)S(1)} %slice.198, f32[4,5,128,1]{3,0,2,1:T(4,128)S(1)} %get-tuple-element.33, f32[4,5,128,1]{3,0,2,1:T(4,128)S(1)} %get-tuple-element.32, f32[4,5,128,1]{3,0,2,1:T(4,128)S(1)} %copy-done.2, f32[4,5,128,128]{3,0,2,1:T(4,128)S(1)} %copy.63, f32[4,5,128,1]{3,0,2,1:T(4,128)S(1)} %copy-done.1), kind=kLoop, calls=%fused_computation.11 | loop fusion | flops 3632640 | bytes 3983360 | tf_op jit(solution)/shard_map/sub | solution.py:74
  33.3 19.5 %all-gather.3.cloned.1.call-done = f32[16,5,128,128]{3,2,1,0:T(8,128)} async-done(((f32[4,5,128,128]{3,2,1,0:T(8,128)}), f32[16,5,128,128]{3,2,1,0:T(8,128)}) %all-gather.3.cloned.1.call-update) | async-done | bytes 5242896 | tf_op jit(solution)/shard_map/all_gather | solution.py:120
  52.7 11.8 %fusion.35 = f32[4,5,128,128]{3,0,2,1:T(4,128)S(1)} fusion(f32[16,5,128,128]{3,2,1,0:T(8,128)} %all-gather.3.cloned.1.call-done, f32[4,5,129,128]{3,0,2,1:T(4,128)} %fusion.30, f32[4,5,128,129]{3,0,2,1:T(4,128)} %fusion.6, f32[16,16]{1,0:T(8,128)S(1)} %fusion.39, s32[]{:T(128)S(6)} %select_n.46, s32[16,16]{1,0:T(8,128)S(1)} %iota_subtract_fusion, ...), kind=kOutput, calls=%fused_computation.47 | convolution fusion | flops 65536576 | bytes 13113348 | tf_op jit(solution)/shard_map/nm,mvjk->nvjk/dot_general | solution.py:117
  64.6 1.2 copy.61
  65.8 1.5 %collective-permute-start.2 = (f32[4,5,1,128]{3,0,2,1:T(4,128)S(1)}, f32[4,5,1,128]{3,0,2,1:T(4,128)S(1)}, u32[]{:S(2)}, u32[]{:S(2)}) collective-permute-start(f32[4,5,1,128]{3,0,2,1:T(4,128)S(1)} %get-tuple-element.39), channel_id=1, source_target_pairs={{0,4},{4,8},{8,12},{12,0},{1,5},{5,9},{9,13},{13,1},{2,6},{6,10},{... | collective-permute-start | bytes 30728 | tf_op jit(solution)/shard_map/ppermute | solution.py:21
  67.3 2.3 %collective-permute-start.3 = (f32[4,5,1,128]{3,0,2,1:T(4,128)S(1)}, f32[4,5,1,128]{3,0,2,1:T(4,128)S(1)}, u32[]{:S(2)}, u32[]{:S(2)}) collective-permute-start(f32[4,5,1,128]{3,0,2,1:T(4,128)S(1)} %get-tuple-element.40), channel_id=1, source_target_pairs={{4,0},{8,4},{12,8},{0,12},{5,1},{9,5},{13,9},{1,13},{6,2},{10,6},{... | collective-permute-start | bytes 30728 | tf_op jit(solution)/shard_map/ppermute | solution.py:22
  69.7 2.3 %fusion.51 = (f32[4,5,128,1]{3,0,2,1:T(4,128)}, f32[4,5,128,1]{3,0,2,1:T(4,128)}) fusion(f32[4,5,128,128]{3,0,2,1:T(4,128)S(1)} %fusion.35), kind=kLoop, calls=%fused_computation.112 | loop fusion | bytes 40960 | tf_op jit(solution)/shard_map/slice | solution.py:84
  72.1 0.8 gather_fusion.2
  73.2 0.8 gather_fusion.3
  74.1 0.3 pad_maximum_fusion.5
  75.6 0.7 fusion.49
  76.4 1.9 %fusion.27 = f32[4,5,129,128]{3,0,2,1:T(4,128)} fusion(f32[4,5,130,128]{3,0,2,1:T(4,128)S(1)} %multiply_dynamic-update-slice_fusion, f32[4,5,1,128]{3,0,2,1:T(4,128)S(1)} %get-tuple-element.49, f32[4,5,128,128]{3,0,2,1:T(4,128)S(1)} %fusion.35, f32[4,5,1,128]{3,0,2,1:T(4,128)S(1)} %get-tuple-element.50, f32[4]{0:T(128)S(1)} %multiply_multiply_fusion), kind=kLoop, calls=%fused_computation.30 | loop fusion | flops 2972160 | bytes 5294096 | tf_op jit(solution)/shard_map/sub | solution.py:74
  78.3 4.3 %fusion.9 = f32[4,5,128,129]{3,0,2,1:T(4,128)} fusion(f32[4,5,128,128]{3,0,2,1:T(4,128)S(1)} %slice.216, f32[4,5,128,1]{3,0,2,1:T(4,128)S(1)} %get-tuple-element.28, f32[4,5,128,1]{3,0,2,1:T(4,128)S(1)} %get-tuple-element.27, f32[4,5,128,1]{3,0,2,1:T(4,128)S(1)} %copy-done.4, f32[4,5,128,128]{3,0,2,1:T(4,128)S(1)} %fusion.35, f32[4,5,128,1]{3,0,2,1:T(4,128)S(1)} %copy-done.3), kind=kLoop, calls=%fused_computation.17 | loop fusion | flops 3632640 | bytes 3983360 | tf_op jit(solution)/shard_map/sub | solution.py:74
  82.6 23.8 %all-gather.5.cloned.1.call-done = f32[16,5,128,128]{3,2,1,0:T(8,128)} async-done(((f32[4,5,128,128]{3,2,1,0:T(8,128)}), f32[16,5,128,128]{3,2,1,0:T(8,128)}) %all-gather.5.cloned.1.call-update) | async-done | bytes 5242896 | tf_op jit(solution)/shard_map/all_gather | solution.py:120
  106.4 11.9 %multiply_add_fusion = (f32[4,5,128,128]{3,0,2,1:T(4,128)S(1)}, f32[4,5,128,128]{3,0,2,1:T(4,128)S(1)}) fusion(f32[4,5,128,128]{3,2,1,0:T(8,128)S(1)} %copy-done, f32[16,5,128,128]{3,2,1,0:T(8,128)} %all-gather.5.cloned.1.call-done, f32[16,16]{1,0:T(8,128)S(1)} %fusion.39, s32[]{:T(128)S(6)} %select_n.46, s32[16,16]{1,0:T(8,128)S(1)} %add_select_fusion, ...), kind=kOutput, calls=%fused_computation.48 | convolution fusion | flops 65536576 | bytes 14424068 | tf_op jit(solution)/shard_map/nm,mvjk->nvjk/dot_general | solution.py:117
  118.3 1.2 copy.64
  119.5 1.2 copy.65
  (59 shorter events, 3.8 us)
Async XLA Ops:
  7.2 7.0 %copy-start = (f32[4,5,128,128]{3,2,1,0:T(8,128)S(1)}, f32[4,5,128,128]{3,2,1,0:T(8,128)}, u32[]{:S(2)}) copy-start(f32[4,5,128,128]{3,2,1,0:T(8,128)} %param.8) | copy-start | bytes 3932164
  7.2 45.6 %all-gather.3.cloned.1.call-start = ((), (), s32[]{:S(2)}) async-start(), calls=%async_computation | async-start | bytes 6553600 | tf_op jit(solution)/shard_map/all_gather | solution.py:120
  7.9 7.7 %copy-start.5 = (s32[1,2,128]{2,1,0:T(2,128)S(1)}, s32[1,2,128]{2,1,0:T(2,128)}, u32[]{:S(2)}) copy-start(s32[1,2,128]{2,1,0:T(2,128)} %param.11) | copy-start | bytes 3076
  7.9 98.5 %all-gather.5.cloned.1.call-start = ((), (), s32[]{:S(2)}) async-start(), calls=%async_computation.1 | async-start | bytes 6553600 | tf_op jit(solution)/shard_map/all_gather | solution.py:120
  8.9 6.8 %copy-start.6 = (s32[4]{0:T(128)S(1)}, s32[4]{0:T(128)}, u32[]{:S(2)}) copy-start(s32[4]{0:T(128)} %param.10) | copy-start | bytes 52
  8.9 7.4 %copy-start.7 = (f32[4]{0:T(128)S(1)}, f32[4]{0:T(128)}, u32[]{:S(2)}) copy-start(f32[4]{0:T(128)} %param.12) | copy-start | bytes 52
  8.9 8.7 %copy-start.8 = (f32[4]{0:T(128)S(1)}, f32[4]{0:T(128)}, u32[]{:S(2)}) copy-start(f32[4]{0:T(128)} %param.13) | copy-start | bytes 52
  8.9 13.6 %collective-permute-start = (f32[4,5,1,128]{3,2,1,0:T(1,128)S(1)}, f32[4,5,1,128]{3,2,1,0:T(1,128)S(1)}, u32[]{:S(2)}, u32[]{:S(2)}) collective-permute-start(f32[4,5,1,128]{3,2,1,0:T(1,128)S(1)} %get-tuple-element.43), channel_id=1, source_target_pairs={{0,4},{4,8},{8,12},{12,0},{1,5},{5,9},{9,13},{13,1},{2,6},{6,10},{... | collective-permute-start | bytes 30728 | tf_op jit(solution)/shard_map/ppermute | solution.py:21
  12.0 11.5 %collective-permute-start.1 = (f32[4,5,1,128]{3,2,1,0:T(1,128)S(1)}, f32[4,5,1,128]{3,2,1,0:T(1,128)S(1)}, u32[]{:S(2)}, u32[]{:S(2)}) collective-permute-start(f32[4,5,1,128]{3,2,1,0:T(1,128)S(1)} %get-tuple-element.44), channel_id=1, source_target_pairs={{4,0},{8,4},{12,8},{0,12},{5,1},{9,5},{13,9},{1,13},{6,2},{10,6},{... | collective-permute-start | bytes 30728 | tf_op jit(solution)/shard_map/ppermute | solution.py:22
  26.9 1.9 %copy-start.1 = (f32[4,5,128,1]{3,0,2,1:T(4,128)S(1)}, f32[4,5,128,1]{3,0,2,1:T(4,128)}, u32[]{:S(2)}) copy-start(f32[4,5,128,1]{3,0,2,1:T(4,128)} %get-tuple-element.41) | copy-start | bytes 30724
  27.0 2.0 %copy-start.2 = (f32[4,5,128,1]{3,0,2,1:T(4,128)S(1)}, f32[4,5,128,1]{3,0,2,1:T(4,128)}, u32[]{:S(2)}) copy-start(f32[4,5,128,1]{3,0,2,1:T(4,128)} %get-tuple-element.42) | copy-start | bytes 30724
  65.8 6.1 %collective-permute-start.2 = (f32[4,5,1,128]{3,0,2,1:T(4,128)S(1)}, f32[4,5,1,128]{3,0,2,1:T(4,128)S(1)}, u32[]{:S(2)}, u32[]{:S(2)}) collective-permute-start(f32[4,5,1,128]{3,0,2,1:T(4,128)S(1)} %get-tuple-element.39), channel_id=1, source_target_pairs={{0,4},{4,8},{8,12},{12,0},{1,5},{5,9},{9,13},{13,1},{2,6},{6,10},{... | collective-permute-start | bytes 30728 | tf_op jit(solution)/shard_map/ppermute | solution.py:21
  67.3 5.6 %collective-permute-start.3 = (f32[4,5,1,128]{3,0,2,1:T(4,128)S(1)}, f32[4,5,1,128]{3,0,2,1:T(4,128)S(1)}, u32[]{:S(2)}, u32[]{:S(2)}) collective-permute-start(f32[4,5,1,128]{3,0,2,1:T(4,128)S(1)} %get-tuple-element.40), channel_id=1, source_target_pairs={{4,0},{8,4},{12,8},{0,12},{5,1},{9,5},{13,9},{1,13},{6,2},{10,6},{... | collective-permute-start | bytes 30728 | tf_op jit(solution)/shard_map/ppermute | solution.py:22
  76.4 1.9 %copy-start.3 = (f32[4,5,128,1]{3,0,2,1:T(4,128)S(1)}, f32[4,5,128,1]{3,0,2,1:T(4,128)}, u32[]{:S(2)}) copy-start(f32[4,5,128,1]{3,0,2,1:T(4,128)} %get-tuple-element.37) | copy-start | bytes 30724
  76.4 1.9 %copy-start.4 = (f32[4,5,128,1]{3,0,2,1:T(4,128)S(1)}, f32[4,5,128,1]{3,0,2,1:T(4,128)}, u32[]{:S(2)}) copy-start(f32[4,5,128,1]{3,0,2,1:T(4,128)} %get-tuple-element.38) | copy-start | bytes 30724
Sparse Core Ops, SparseCore 0:
  9.6 43.1 all-gather.2
  65.9 40.4 all-gather.4
where the time goes:
time: 128 us
  waiting for transfers between devices  43.9 us (34%)
  matrix products  23.7 us (19%)
  other arithmetic  19.8 us (15%)
  local copies, waits for them, and re-layouts  15.9 us (12%)
  between operations  15.1 us (12%)
  starting transfers between devices  9.12 us (7%)
    all_gather x2, waiting for transfers between devices, spectral_of(): lax.all_gather(field, 'inst', axis=0, tiled=True)  43.2 us
    dot_general x2, matrix products, spectral_of(): jnp.einsum('nm,mvjk->nvjk', own_rows, lax.all_gather(field, 'inst', axis=...  23.7 us
    sub x4, other arithmetic, face_terms(): 0.5 * (flux_left + flux_right) - speed * 0.5 * (left + right)  12.4 us
    ppermute x2, starting transfers between devices, padded_2(): before = lax.ppermute(last, axis, up)  4.62 us
    slice x2, local copies, waits for them, and re-layouts, local_residual(): field[..., :1]  4.51 us
    ppermute x2, starting transfers between devices, padded_2(): after = lax.ppermute(initial, axis, down)  4.43 us
    unnamed x23, local copies, waits for them, and re-layouts  3.41 us
  transfers between devices with their start and end apart: 6, of which 2 were waited for; matrix products, arithmetic and copies ran while one was open for 25% of the time, Pallas kernels for 0%

commit v1 on v0

--- a/solution.py
+++ b/solution.py
@@ -114,10 +114,37 @@
     own_rows = lax.dynamic_slice_in_dim(matrix, own_start, per_dev, 0)
 
     def spectral_of(field):
+
+        def mix_the_vectors(local_array, axis_name):
+            plain = lax.axis_size(axis_name)
+            piece_next = lax.axis_index(axis_name)
+            arr_now, res, left_arr = (plain, piece_next, local_array.shape[0])
+            trail = [m * arr_now if at == 0 else m for at, m in enumerate(local_array.shape)]
+            back = jnp.zeros(trail, local_array.dtype)
+            big = found_now = local_array
+            d = 1
+            w2 = lax.dynamic_update_slice_in_dim(back, local_array, res * left_arr, axis=0)
+            while d < arr_now // 2 + 1:
+                big = lax.ppermute(
+                    big, axis_name, [(at, (at + 1) % arr_now) for at in range(arr_now)]
+                )
+                w2 = lax.dynamic_update_slice_in_dim(
+                    w2, big, (res - d) % arr_now * left_arr, axis=0
+                )
+                if 2 * d < arr_now:
+                    found_now = lax.ppermute(
+                        found_now, axis_name, [(at, (at - 1) % arr_now) for at in range(arr_now)]
+                    )
+                    w2 = lax.dynamic_update_slice_in_dim(
+                        w2, found_now, (res + d) % arr_now * left_arr, axis=0
+                    )
+                d = d + 1
+            return w2
+
         return jnp.einsum(
             "nm,mvjk->nvjk",
             own_rows,
-            lax.all_gather(field, "inst", axis=0, tiled=True),
+            mix_the_vectors(field, "inst"),
             precision=lax.Precision.HIGHEST,
         )
 

time: 128 us -> 116 us (0.906)
  local copies, waits for them, and re-layouts: 15.9 us -> 33.8 us
  between operations: 15.1 us -> 1.74 us
  matrix products: 23.7 us -> 12 us
  waiting for transfers between devices: 43.9 us -> 34.4 us
  starting transfers between devices: 9.12 us -> 16 us
  other arithmetic: 19.8 us -> 18.1 us
    all_gather x2 -> x0, waiting for transfers between devices: 43.2 us -> none  [spectral_of(): lax.all_gather(field, 'inst', axis=0, tiled=True)]
    ppermute x0 -> x6, waiting for transfers between devices: none -> 34.4 us  [the longest x4 34.4 us: mix_the_vectors(): lax.ppermute(big, axis_name, [(at, (at + 1) % arr_now) for at in range(ar...]
    dynamic_update_slice x0 -> x6, local copies, waits for them, and re-layouts: none -> 12.2 us  [the longest x4 7.24 us: mix_the_vectors(): lax.dynamic_update_slice_in_dim(w2, big, (res - d) % arr_now * left_arr,...]
    dot_general x2, matrix products: 23.7 us -> 12 us  [spectral_of(): jnp.einsum('nm,mvjk->nvjk', own_rows, mix_the_vectors(field, 'inst'), pre...]
    ppermute x0 -> x6, starting transfers between devices: none -> 7.69 us  [the longest x4 5.64 us: mix_the_vectors(): lax.ppermute(big, axis_name, [(at, (at + 1) % arr_now) for at in range(ar...]
    sub x4, other arithmetic: 12.4 us -> 8.2 us  [face_terms(): 0.5 * (flux_left + flux_right) - speed * 0.5 * (left + right)]
    unnamed x23 -> x21, local copies, waits for them, and re-layouts: 3.41 us -> 7.05 us
    another operation x0 -> x2, local copies, waits for them, and re-layouts: none -> 3.22 us
  transfers between devices with their start and end apart: 6 -> 10, of which waited for: 2 -> 4; matrix products, arithmetic and copies ran while one was open for 25% -> 38% of each run, Pallas kernels for 0% -> 0%
where the time goes in v1:
time: 116 us
  waiting for transfers between devices  34.4 us (30%)
  local copies, waits for them, and re-layouts  33.8 us (29%)
  other arithmetic  18.1 us (16%)
  starting transfers between devices  16 us (14%)
  matrix products  12 us (10%)
  between operations  1.74 us (2%)
    ppermute x4, waiting for transfers between devices, mix_the_vectors(): lax.ppermute(big, axis_name, [(at, (at + 1) % arr_now) for at in range(ar...  34.4 us
    dot_general x2, matrix products, spectral_of(): jnp.einsum('nm,mvjk->nvjk', own_rows, mix_the_vectors(field, 'inst'), pre...  12 us
    sub x4, other arithmetic, face_terms(): 0.5 * (flux_left + flux_right) - speed * 0.5 * (left + right)  8.2 us
    dynamic_update_slice x4, local copies, waits for them, and re-layouts, mix_the_vectors(): lax.dynamic_update_slice_in_dim(w2, big, (res - d) % arr_now * left_arr,...  7.24 us
    unnamed x21, local copies, waits for them, and re-layouts  7.05 us
    ppermute x4, starting transfers between devices, mix_the_vectors(): lax.ppermute(big, axis_name, [(at, (at + 1) % arr_now) for at in range(ar...  5.64 us
    dynamic_update_slice x2, local copies, waits for them, and re-layouts, mix_the_vectors(): lax.dynamic_update_slice_in_dim(w2, found_now, (res + d) % arr_now * left...  4.96 us
    ppermute x2, starting transfers between devices, padded_2(): after = lax.ppermute(initial, axis, down)  4.86 us
  transfers between devices with their start and end apart: 10, of which 4 were waited for; matrix products, arithmetic and copies ran while one was open for 38% of the time, Pallas kernels for 0%

profile of v1, /device:TPU:0, one launch (start us, length us, event | category | flops | bytes accessed | tf_op | source)
XLA Modules:
  0.0 116.0 jit_solution(16949332957205578946)
XLA Ops:
  1.1 2.0 %collective-permute-start.3 = (f32[4,5,128,128]{3,2,1,0:T(8,128)}, f32[4,5,128,128]{3,2,1,0:T(8,128)}, u32[]{:S(2)}, u32[]{:S(2)}) collective-permute-start(f32[4,5,128,128]{3,2,1,0:T(8,128)} %param.8), channel_id=1, source_target_pairs={{0,3},{1,0},{2,1},{3,2},{4,7},{5,4},{6,5},{7,6},{8,11},{9,8},{10,9... | collective-permute-start | bytes 3932168 | tf_op jit(solution)/shard_map/ppermute | solution.py:135
  3.1 1.0 fusion.39
  4.1 2.4 %collective-permute-start = (f32[4,5,1,128]{3,2,1,0:T(1,128)S(1)}, f32[4,5,1,128]{3,2,1,0:T(1,128)S(1)}, u32[]{:S(2)}, u32[]{:S(2)}) collective-permute-start(f32[4,5,1,128]{3,2,1,0:T(1,128)S(1)} %get-tuple-element.41), channel_id=1, source_target_pairs={{0,4},{4,8},{8,12},{12,0},{1,5},{5,9},{9,13},{13,1},{2,6},{6,10},{... | collective-permute-start | bytes 30728 | tf_op jit(solution)/shard_map/ppermute | solution.py:21
  6.5 2.1 %collective-permute-start.1 = (f32[4,5,1,128]{3,2,1,0:T(1,128)S(1)}, f32[4,5,1,128]{3,2,1,0:T(1,128)S(1)}, u32[]{:S(2)}, u32[]{:S(2)}) collective-permute-start(f32[4,5,1,128]{3,2,1,0:T(1,128)S(1)} %get-tuple-element.42), channel_id=1, source_target_pairs={{4,0},{8,4},{12,8},{0,12},{5,1},{9,5},{13,9},{1,13},{6,2},{10,6},{... | collective-permute-start | bytes 30728 | tf_op jit(solution)/shard_map/ppermute | solution.py:22
  9.2 1.3 %fusion.31 = s32[]{:T(128)} fusion(s32[4]{0:T(128)} %param.10, s32[]{:T(128)} %bitcast.42), kind=kLoop, calls=%fused_computation.115 | loop fusion | flops 11 | bytes 24 | tf_op jit(solution)/shard_map/reduce_sum | solution.py:106
  10.5 2.0 %fusion.30 = f32[]{:T(128)} fusion(f32[4]{0:T(128)} %param.13, s32[]{:T(128)} %fusion.31), kind=kLoop, calls=%fused_computation.114 | loop fusion | flops 11 | bytes 24 | tf_op jit(solution)/shard_map/reduce_sum | solution.py:109
  12.5 1.9 %fusion.29 = f32[]{:T(128)} fusion(f32[4]{0:T(128)} %param.12, s32[]{:T(128)} %fusion.31), kind=kLoop, calls=%fused_computation.113 | loop fusion | flops 11 | bytes 24 | tf_op jit(solution)/shard_map/reduce_sum | solution.py:108
  15.2 2.8 %broadcast.105.clone = f32[16,5,128,128]{3,0,2,1:T(8,128)} broadcast(f32[]{:T(128)} %constant.75.clone.1), dimensions={} | broadcast | bytes 5242884 | tf_op jit(solution)/shard_map/broadcast.21
  18.0 2.1 %fusion.40 = (f32[4,5,128,128]{3,0,2,1:T(4,128)S(1)}, f32[16,5,128,128]{3,0,2,1:T(8,128)}) fusion(f32[4,5,128,128]{3,2,1,0:T(8,128)S(1)} %copy-done.1, f32[16,5,128,128]{3,0,2,1:T(8,128)} %broadcast.105.clone, s32[]{:T(128)S(6)} %select_n.80), kind=kLoop, calls=%fused_computation.123 | loop fusion | bytes 3932164 | tf_op args[0]
  20.1 2.2 %fusion.38 = (f32[4,5,128,1]{3,0,2,1:T(4,128)}, f32[4,5,128,1]{3,0,2,1:T(4,128)}) fusion(f32[4,5,128,128]{3,0,2,1:T(4,128)S(1)} %get-tuple-element.43), kind=kLoop, calls=%fused_computation.121 | loop fusion | bytes 40960 | tf_op jit(solution)/shard_map/slice | solution.py:84
  22.3 1.2 %multiply_multiply_fusion = f32[4]{0:T(128)S(1)} fusion(f32[]{:T(128)} %fusion.30, s32[]{:T(128)S(6)} %mul.304, f32[]{:T(128)} %fusion.29), kind=kLoop, calls=%fused_computation.116 | loop fusion | flops 24 | bytes 28 | tf_op jit(solution)/shard_map/mul | solution.py:75
  27.9 2.1 %collective-permute-done.2 = f32[4,5,128,128]{3,2,1,0:T(8,128)} collective-permute-done((f32[4,5,128,128]{3,2,1,0:T(8,128)}, f32[4,5,128,128]{3,2,1,0:T(8,128)}, u32[]{:S(2)}, u32[]{:S(2)}) %collective-permute-start.2) | collective-permute-done | bytes 1310752 | tf_op jit(solution)/shard_map/ppermute | solution.py:128
  30.1 2.5 %collective-permute-start.4 = (f32[4,5,128,128]{3,2,1,0:T(8,128)}, f32[4,5,128,128]{3,2,1,0:T(8,128)S(1)}, u32[]{:S(2)}, u32[]{:S(2)}) collective-permute-start(f32[4,5,128,128]{3,2,1,0:T(8,128)} %collective-permute-done.2), channel_id=1, source_target_pairs={{0,1},{1,2},{2,3},{3,0},{4,5},{5,6},{6,7},{7,4},{8,9},{9,10},{10,1... | collective-permute-start | bytes 3932168 | tf_op jit(solution)/shard_map/ppermute | solution.py:128
  33.4 1.2 %copy-done.2 = f32[4,5,128,1]{3,0,2,1:T(4,128)S(1)} copy-done((f32[4,5,128,1]{3,0,2,1:T(4,128)S(1)}, f32[4,5,128,1]{3,0,2,1:T(4,128)}, u32[]{:S(2)}) %copy-start.2) | copy-done | bytes 10264
  35.0 3.4 %fusion.2 = f32[4,5,128,129]{3,0,2,1:T(4,128)S(1)} fusion(f32[4,5,128,128]{3,0,2,1:T(4,128)S(1)} %slice.198, f32[4,5,128,1]{3,0,2,1:T(4,128)S(1)} %get-tuple-element.31, f32[4,5,128,1]{3,0,2,1:T(4,128)S(1)} %get-tuple-element.30, f32[4,5,128,1]{3,0,2,1:T(4,128)S(1)} %copy-done.3, f32[4,5,128,128]{3,0,2,1:T(4,128)S(1)} %get-tuple-element.43, ...), kind=kLoop, calls=%fused_computation.7 | loop fusion | flops 3632640 | bytes 3983360 | tf_op jit(solution)/shard_map/sub | solution.py:74
  38.4 3.3 %copy_dynamic-update-slice_fusion.2 = f32[16,5,128,128]{3,0,2,1:T(8,128)} fusion(f32[16,5,128,128]{3,0,2,1:T(8,128)} %get-tuple-element.44, s32[]{:T(128)S(6)} %select_n.82, f32[4,5,128,128]{3,2,1,0:T(8,128)} %collective-permute-done.2), kind=kLoop, calls=%fused_computation.46 | loop fusion | bytes 2621444 | tf_op jit(solution)/shard_map/dynamic_update_slice | solution.py:131
  41.7 3.3 %copy_dynamic-update-slice_fusion.1 = f32[16,5,128,128]{3,0,2,1:T(8,128)} fusion(f32[16,5,128,128]{3,0,2,1:T(8,128)} %copy_dynamic-update-slice_fusion.2, s32[]{:T(128)S(6)} %select_n.84, f32[4,5,128,128]{3,2,1,0:T(8,128)} %collective-permute-done.3), kind=kLoop, calls=%fused_computation.45 | loop fusion | bytes 2621444 | tf_op jit(solution)/shard_map/dynamic_update_slice | solution.py:138
  45.0 2.3 %collective-permute-done.4 = f32[4,5,128,128]{3,2,1,0:T(8,128)S(1)} collective-permute-done((f32[4,5,128,128]{3,2,1,0:T(8,128)}, f32[4,5,128,128]{3,2,1,0:T(8,128)S(1)}, u32[]{:S(2)}, u32[]{:S(2)}) %collective-permute-start.4) | collective-permute-done | bytes 1310752 | tf_op jit(solution)/shard_map/ppermute | solution.py:128
  47.3 2.0 %copy_dynamic-update-slice_fusion = f32[16,5,128,128]{3,0,2,1:T(8,128)} fusion(f32[16,5,128,128]{3,0,2,1:T(8,128)} %copy_dynamic-update-slice_fusion.1, s32[]{:T(128)S(6)} %select_n.86, f32[4,5,128,128]{3,2,1,0:T(8,128)S(1)} %collective-permute-done.4), kind=kLoop, calls=%fused_computation.44 | loop fusion | bytes 2621444 | tf_op jit(solution)/shard_map/dynamic_update_slice | solution.py:131
  49.8 7.2 %constant_dynamic-update-slice_fusion.3 = (f32[16,5,128,128]{3,0,2,1:T(8,128)S(1)}, f32[4,5,128,128]{3,0,2,1:T(4,128)S(1)}) fusion(f32[16,5,128,128]{3,0,2,1:T(8,128)S(1)} %broadcast.105, s32[]{:T(128)S(6)} %select_n.80, f32[16,5,128,128]{3,0,2,1:T(8,128)} %copy_dynamic-update-slice_fusion, f32[16,16]{1,0:T(8,128)S(1)} %fusion.21, ...), kind=kOutput, calls=%fused_computation.97 | convolution fusion | flops 65536576 | bytes 14425088 | tf_op jit(solution)/shard_map/nm,mvjk->nvjk/dot_general | solution.py:144
  57.0 2.6 %collective-permute-start.7 = (f32[4,5,128,128]{3,0,2,1:T(4,128)S(1)}, f32[4,5,128,128]{3,0,2,1:T(4,128)}, u32[]{:S(2)}, u32[]{:S(2)}) collective-permute-start(f32[4,5,128,128]{3,0,2,1:T(4,128)S(1)} %get-tuple-element.48), channel_id=1, source_target_pairs={{0,1},{1,2},{2,3},{3,0},{4,5},{5,6},{6,7},{7,4},{8,9},{9,10},{10,1... | collective-permute-start | bytes 3932168 | tf_op jit(solution)/shard_map/ppermute | solution.py:128
  59.6 1.1 collective-permute-start.5
  60.7 2.8 %collective-permute-start.6 = (f32[4,5,1,128]{3,0,2,1:T(4,128)S(1)}, f32[4,5,1,128]{3,0,2,1:T(4,128)S(1)}, u32[]{:S(2)}, u32[]{:S(2)}) collective-permute-start(f32[4,5,1,128]{3,0,2,1:T(4,128)S(1)} %get-tuple-element.38), channel_id=1, source_target_pairs={{4,0},{8,4},{12,8},{0,12},{5,1},{9,5},{13,9},{1,13},{6,2},{10,6},{... | collective-permute-start | bytes 30728 | tf_op jit(solution)/shard_map/ppermute | solution.py:22
  63.5 2.2 %fusion.36 = (f32[4,5,128,1]{3,0,2,1:T(4,128)}, f32[4,5,128,1]{3,0,2,1:T(4,128)}) fusion(f32[4,5,128,128]{3,0,2,1:T(4,128)S(1)} %get-tuple-element.48), kind=kLoop, calls=%fused_computation.119 | loop fusion | bytes 40960 | tf_op jit(solution)/shard_map/slice | solution.py:84
  69.9 21.3 %collective-permute-done.7 = f32[4,5,128,128]{3,0,2,1:T(4,128)} collective-permute-done((f32[4,5,128,128]{3,0,2,1:T(4,128)S(1)}, f32[4,5,128,128]{3,0,2,1:T(4,128)}, u32[]{:S(2)}, u32[]{:S(2)}) %collective-permute-start.7) | collective-permute-done | bytes 1310752 | tf_op jit(solution)/shard_map/ppermute | solution.py:128
  93.0 3.4 %fusion.5 = f32[4,5,128,129]{3,0,2,1:T(4,128)S(1)} fusion(f32[4,5,128,128]{3,0,2,1:T(4,128)S(1)} %slice.216, f32[4,5,128,1]{3,0,2,1:T(4,128)S(1)} %get-tuple-element.26, f32[4,5,128,1]{3,0,2,1:T(4,128)S(1)} %get-tuple-element.25, f32[4,5,128,1]{3,0,2,1:T(4,128)S(1)} %copy-done.5, f32[4,5,128,128]{3,0,2,1:T(4,128)S(1)} %get-tuple-element.48, ...), kind=kLoop, calls=%fused_computation.13 | loop fusion | flops 3632640 | bytes 3983360 | tf_op jit(solution)/shard_map/sub | solution.py:74
  96.4 1.6 %constant_dynamic-update-slice_fusion.2 = f32[16,5,128,128]{3,0,2,1:T(8,128)S(1)} fusion(f32[16,5,128,128]{3,0,2,1:T(8,128)S(1)} %bitcast.44, f32[4,5,128,128]{3,0,2,1:T(4,128)} %collective-permute-done.7, s32[]{:T(128)S(6)} %select_n.82), kind=kLoop, calls=%fused_computation.96 | loop fusion | bytes 2621444 | tf_op jit(solution)/shard_map/dynamic_update_slice | solution.py:131
  98.1 1.6 %constant_dynamic-update-slice_fusion.1 = f32[16,5,128,128]{3,0,2,1:T(8,128)S(1)} fusion(f32[16,5,128,128]{3,0,2,1:T(8,128)S(1)} %constant_dynamic-update-slice_fusion.2, f32[4,5,128,128]{3,0,2,1:T(4,128)} %collective-permute-done.8, s32[]{:T(128)S(6)} %select_n.84), kind=kLoop, calls=%fused_computation.95 | loop fusion | bytes 2621444 | tf_op jit(solution)/shard_map/dynamic_update_slice | solution.py:138
  99.7 8.7 %collective-permute-done.9 = f32[4,5,128,128]{3,0,2,1:T(4,128)S(1)} collective-permute-done((f32[4,5,128,128]{3,0,2,1:T(4,128)}, f32[4,5,128,128]{3,0,2,1:T(4,128)S(1)}, u32[]{:S(2)}, u32[]{:S(2)}) %collective-permute-start.9) | collective-permute-done | bytes 1310752 | tf_op jit(solution)/shard_map/ppermute | solution.py:128
  108.7 4.9 %multiply_add_fusion = (f32[4,5,128,128]{3,0,2,1:T(4,128)S(1)}, f32[4,5,128,128]{3,0,2,1:T(4,128)S(1)}) fusion(f32[4,5,128,128]{3,2,1,0:T(8,128)S(1)} %copy-done.1, f32[16,5,128,128]{3,0,2,1:T(8,128)S(1)} %constant_dynamic-update-slice_fusion, f32[16,16]{1,0:T(8,128)S(1)} %fusion.21, s32[]{:T(128)S(6)} %select_n.80, s32[16,16]{1,0:T(8,128)S(1)} %add_select_fusion, ...), kind=kOutput, calls=%fused_computation.47 | convolution fusion | flops 65536576 | bytes 14424068 | tf_op jit(solution)/shard_map/nm,mvjk->nvjk/dot_general | solution.py:144
  113.6 1.2 %copy.46 = f32[4,5,128,128]{3,2,1,0:T(8,128)} copy(f32[4,5,128,128]{3,0,2,1:T(4,128)S(1)} %get-tuple-element.49) | data formatting | bytes 2621440
  114.8 1.2 %copy.47 = f32[4,5,128,128]{3,2,1,0:T(8,128)} copy(f32[4,5,128,128]{3,0,2,1:T(4,128)S(1)} %get-tuple-element.50) | data formatting | bytes 2621440
  (71 shorter events, 13.5 us)
Async XLA Ops:
  0.6 29.4 %collective-permute-start.2 = (f32[4,5,128,128]{3,2,1,0:T(8,128)}, f32[4,5,128,128]{3,2,1,0:T(8,128)}, u32[]{:S(2)}, u32[]{:S(2)}) collective-permute-start(f32[4,5,128,128]{3,2,1,0:T(8,128)} %param.8), channel_id=1, source_target_pairs={{0,1},{1,2},{2,3},{3,0},{4,5},{5,6},{6,7},{7,4},{8,9},{9,10},{10,1... | collective-permute-start | bytes 3932168 | tf_op jit(solution)/shard_map/ppermute | solution.py:128
  1.1 40.6 %collective-permute-start.3 = (f32[4,5,128,128]{3,2,1,0:T(8,128)}, f32[4,5,128,128]{3,2,1,0:T(8,128)}, u32[]{:S(2)}, u32[]{:S(2)}) collective-permute-start(f32[4,5,128,128]{3,2,1,0:T(8,128)} %param.8), channel_id=1, source_target_pairs={{0,3},{1,0},{2,1},{3,2},{4,7},{5,4},{6,5},{7,6},{8,11},{9,8},{10,9... | collective-permute-start | bytes 3932168 | tf_op jit(solution)/shard_map/ppermute | solution.py:135
  4.1 20.6 %collective-permute-start = (f32[4,5,1,128]{3,2,1,0:T(1,128)S(1)}, f32[4,5,1,128]{3,2,1,0:T(1,128)S(1)}, u32[]{:S(2)}, u32[]{:S(2)}) collective-permute-start(f32[4,5,1,128]{3,2,1,0:T(1,128)S(1)} %get-tuple-element.41), channel_id=1, source_target_pairs={{0,4},{4,8},{8,12},{12,0},{1,5},{5,9},{9,13},{13,1},{2,6},{6,10},{... | collective-permute-start | bytes 30728 | tf_op jit(solution)/shard_map/ppermute | solution.py:21
  6.5 17.1 %collective-permute-start.1 = (f32[4,5,1,128]{3,2,1,0:T(1,128)S(1)}, f32[4,5,1,128]{3,2,1,0:T(1,128)S(1)}, u32[]{:S(2)}, u32[]{:S(2)}) collective-permute-start(f32[4,5,1,128]{3,2,1,0:T(1,128)S(1)} %get-tuple-element.42), channel_id=1, source_target_pairs={{4,0},{8,4},{12,8},{0,12},{5,1},{9,5},{13,9},{1,13},{6,2},{10,6},{... | collective-permute-start | bytes 30728 | tf_op jit(solution)/shard_map/ppermute | solution.py:22
  15.2 2.8 %copy-start.1 = (f32[4,5,128,128]{3,2,1,0:T(8,128)S(1)}, f32[4,5,128,128]{3,2,1,0:T(8,128)}, u32[]{:S(2)}) copy-start(f32[4,5,128,128]{3,2,1,0:T(8,128)} %param.8) | copy-start | bytes 3932164
  30.1 17.2 %collective-permute-start.4 = (f32[4,5,128,128]{3,2,1,0:T(8,128)}, f32[4,5,128,128]{3,2,1,0:T(8,128)S(1)}, u32[]{:S(2)}, u32[]{:S(2)}) collective-permute-start(f32[4,5,128,128]{3,2,1,0:T(8,128)} %collective-permute-done.2), channel_id=1, source_target_pairs={{0,1},{1,2},{2,3},{3,0},{4,5},{5,6},{6,7},{7,4},{8,9},{9,10},{10,1... | collective-permute-start | bytes 3932168 | tf_op jit(solution)/shard_map/ppermute | solution.py:128
  33.3 1.3 %copy-start.2 = (f32[4,5,128,1]{3,0,2,1:T(4,128)S(1)}, f32[4,5,128,1]{3,0,2,1:T(4,128)}, u32[]{:S(2)}) copy-start(f32[4,5,128,1]{3,0,2,1:T(4,128)} %get-tuple-element.39) | copy-start | bytes 30724
  33.3 1.7 %copy-start.3 = (f32[4,5,128,1]{3,0,2,1:T(4,128)S(1)}, f32[4,5,128,1]{3,0,2,1:T(4,128)}, u32[]{:S(2)}) copy-start(f32[4,5,128,1]{3,0,2,1:T(4,128)} %get-tuple-element.40) | copy-start | bytes 30724
  56.9 8.8 %copy-start = (f32[16,5,128,128]{3,0,2,1:T(8,128)}, f32[16,5,128,128]{3,0,2,1:T(8,128)S(1)}, u32[]{:S(2)}) copy-start(f32[16,5,128,128]{3,0,2,1:T(8,128)S(1)} %get-tuple-element.47) | copy-start | bytes 15728644
  57.0 41.1 %collective-permute-start.8 = (f32[4,5,128,128]{3,0,2,1:T(4,128)S(1)}, f32[4,5,128,128]{3,0,2,1:T(4,128)}, u32[]{:S(2)}, u32[]{:S(2)}) collective-permute-start(f32[4,5,128,128]{3,0,2,1:T(4,128)S(1)} %get-tuple-element.48), channel_id=1, source_target_pairs={{0,3},{1,0},{2,1},{3,2},{4,7},{5,4},{6,5},{7,6},{8,11},{9,8},{10,9... | collective-permute-start | bytes 3932168 | tf_op jit(solution)/shard_map/ppermute | solution.py:135
  57.0 34.2 %collective-permute-start.7 = (f32[4,5,128,128]{3,0,2,1:T(4,128)S(1)}, f32[4,5,128,128]{3,0,2,1:T(4,128)}, u32[]{:S(2)}, u32[]{:S(2)}) collective-permute-start(f32[4,5,128,128]{3,0,2,1:T(4,128)S(1)} %get-tuple-element.48), channel_id=1, source_target_pairs={{0,1},{1,2},{2,3},{3,0},{4,5},{5,6},{6,7},{7,4},{8,9},{9,10},{10,1... | collective-permute-start | bytes 3932168 | tf_op jit(solution)/shard_map/ppermute | solution.py:128
  59.6 7.1 %collective-permute-start.5 = (f32[4,5,1,128]{3,0,2,1:T(4,128)S(1)}, f32[4,5,1,128]{3,0,2,1:T(4,128)S(1)}, u32[]{:S(2)}, u32[]{:S(2)}) collective-permute-start(f32[4,5,1,128]{3,0,2,1:T(4,128)S(1)} %get-tuple-element.37), channel_id=1, source_target_pairs={{0,4},{4,8},{8,12},{12,0},{1,5},{5,9},{9,13},{13,1},{2,6},{6,10},{... | collective-permute-start | bytes 30728 | tf_op jit(solution)/shard_map/ppermute | solution.py:21
  60.7 5.0 %collective-permute-start.6 = (f32[4,5,1,128]{3,0,2,1:T(4,128)S(1)}, f32[4,5,1,128]{3,0,2,1:T(4,128)S(1)}, u32[]{:S(2)}, u32[]{:S(2)}) collective-permute-start(f32[4,5,1,128]{3,0,2,1:T(4,128)S(1)} %get-tuple-element.38), channel_id=1, source_target_pairs={{4,0},{8,4},{12,8},{0,12},{5,1},{9,5},{13,9},{1,13},{6,2},{10,6},{... | collective-permute-start | bytes 30728 | tf_op jit(solution)/shard_map/ppermute | solution.py:22
  91.2 17.2 %collective-permute-start.9 = (f32[4,5,128,128]{3,0,2,1:T(4,128)}, f32[4,5,128,128]{3,0,2,1:T(4,128)S(1)}, u32[]{:S(2)}, u32[]{:S(2)}) collective-permute-start(f32[4,5,128,128]{3,0,2,1:T(4,128)} %collective-permute-done.7), channel_id=1, source_target_pairs={{0,1},{1,2},{2,3},{3,0},{4,5},{5,6},{6,7},{7,4},{8,9},{9,10},{10,1... | collective-permute-start | bytes 3932168 | tf_op jit(solution)/shard_map/ppermute | solution.py:128
  91.3 1.3 %copy-start.4 = (f32[4,5,128,1]{3,0,2,1:T(4,128)S(1)}, f32[4,5,128,1]{3,0,2,1:T(4,128)}, u32[]{:S(2)}) copy-start(f32[4,5,128,1]{3,0,2,1:T(4,128)} %get-tuple-element.35) | copy-start | bytes 30724
  91.3 1.7 %copy-start.5 = (f32[4,5,128,1]{3,0,2,1:T(4,128)S(1)}, f32[4,5,128,1]{3,0,2,1:T(4,128)}, u32[]{:S(2)}) copy-start(f32[4,5,128,1]{3,0,2,1:T(4,128)} %get-tuple-element.36) | copy-start | bytes 30724
  91.4 5.0 %slice-start = ((s8[5242880]{0:T(1024)(128)(4,1)}), s8[4194304]{0:T(1024)(128)(4,1)S(1)}, s32[]{:S(2)}) async-start(s8[5242880]{0:T(1024)(128)(4,1)} %bitcast.43), calls=%async_computation | async-start | bytes 8388608
  93.0 3.4 %slice-start.1 = ((s8[5242880]{0:T(1024)(128)(4,1)}), s8[1048576]{0:T(1024)(128)(4,1)S(1)}, s32[]{:S(2)}) async-start(s8[5242880]{0:T(1024)(128)(4,1)} %bitcast.43), calls=%async_computation.1 | async-start | bytes 2097152
